TPU v7x, 32 devices: a whole 2x2x4 slice. The times are simulated.
32 devices in a mesh: band: 16 (over z, y, x), chan: 2 (over core).
Axes of the slice: x: 2, y: 2, z: 4, core: 2. Of those that a mesh axis runs over, the one named last changes fastest.
Arguments:
- latent: bfloat16 [384, 48, 1440], P(None, 'band'), may hold values from -6 to 6
- decoder_weight: bfloat16 [42, 384], P('chan'), may hold values from -0.3125 to 0.3125
- target: bfloat16 [42, 48, 1440], P('chan', 'band'), may hold values from -6 to 6
Outputs:
- grad_latent: bfloat16 [384, 48, 1440], P('chan', 'band')
- grad_weight: float32 [42, 384], P('chan')
- loss_spectrum: float32 [42, 721], P('chan')
All inputs are finite; a program needn't handle non-finite values.
Results may differ from a plain program's by a relative error of at most 0.0077.
Values may be sent and summed in bfloat16 or wider, within the bound.
A program may use at most 128 MiB of HBM per device.

v0:
```python
import math

import jax
import jax.numpy as jnp
from jax import lax
from jax.sharding import PartitionSpec as P

NLON = 1440
TRUNC = 720
MPAD = 768
NL = 721
NLP = 768


def fourier_table(order_ids):
    longitude = jnp.arange(NLON)
    phase_index = longitude[:, None] * order_ids[None, :] % NLON
    angles = 2.0 * math.pi / NLON * phase_index.astype(jnp.float32)
    in_range = (order_ids <= TRUNC)[None, :]
    norm_scale = 1.0 / math.sqrt(NLON)
    cosines = jnp.where(in_range, jnp.cos(angles) * norm_scale, 0.0)
    negsines = jnp.where(in_range, -jnp.sin(angles) * norm_scale, 0.0)
    return jnp.stack([cosines, negsines], axis=1).astype(jnp.bfloat16)


def legendre_rows(order_ids, lat_count, row_total, cutoff):
    lat_index = jnp.arange(lat_count).astype(jnp.float32)
    colatitude = math.pi * (lat_index + 0.5) / lat_count
    cosines = jnp.cos(colatitude)
    colat_sin = jnp.sin(colatitude)
    weights = math.sqrt(math.pi / lat_count) * colat_sin
    order_float = order_ids.astype(jnp.float32)[:, None]
    log_start = (
        0.5 * jnp.log(order_float + 0.5)
        + lax.lgamma(order_float + 0.5)
        - lax.lgamma(order_float + 1.0)
        - 0.5 * math.log(math.pi)
        + order_float * jnp.log(colat_sin)[None, :]
    )
    zero_rows = jnp.zeros((order_ids.shape[0], lat_count), jnp.float32)

    def advance(carried, offset):
        before, current, log_scale = carried
        scaled = current * jnp.exp(log_scale)
        degree = order_float + offset.astype(jnp.float32) + 1.0
        previous_degree = degree - 1.0
        factor = jnp.sqrt(
            (4.0 * degree * degree - 1.0) / (degree * degree - order_float * order_float)
        )
        back_factor = jnp.sqrt(
            jnp.maximum(previous_degree * previous_degree - order_float * order_float, 0.0)
            / (4.0 * previous_degree * previous_degree - 1.0)
        )
        following = factor * (cosines[None, :] * current - back_factor * before)
        magnitude = jnp.sqrt(current * current + following * following)
        return (
            (current / magnitude, following / magnitude, log_scale + jnp.log(magnitude)),
            scaled,
        )

    initial = (zero_rows, zero_rows + 1.0, log_start)
    _, stacked = lax.scan(advance, initial, jnp.arange(row_total), unroll=4)
    degrees = jnp.arange(row_total)[:, None] + order_ids[None, :]
    inside = (degrees <= cutoff)[:, :, None]
    return jnp.where(inside, stacked * weights[None, None, :], 0.0).astype(jnp.bfloat16)


def spectral_terms(power_pred, power_true, cross_power):
    first_power = power_pred + 1.0
    second_power = power_true + 1.0
    first_root = jnp.sqrt(first_power)
    second_root = jnp.sqrt(second_power)
    joint_root = first_root * second_root
    coherence = cross_power / joint_root
    combined = first_power + second_power
    loss_terms = jnp.square(first_root - second_root) + combined * (1.0 - coherence)
    d_power = (
        2.0
        - second_root / first_root
        - coherence
        + combined * cross_power / (2.0 * first_power * joint_root)
    )
    d_cross = -combined / joint_root
    return (loss_terms, d_power, d_cross)


def local(latent, decoder_weight, target):
    bands = lax.axis_size("band")
    band_index = lax.axis_index("band")
    band_partition = MPAD // bands
    latitude_rows = target.shape[1]
    channels = target.shape[0]
    latent_width = latent.shape[0]
    cell_count = latitude_rows * NLON
    slot_ids = jnp.arange(MPAD)
    resident_orders = lax.dynamic_slice_in_dim(
        slot_ids, band_index * band_partition, band_partition, 0
    )
    flat_latent = latent.reshape(latent_width, cell_count)
    predicted = jnp.dot(decoder_weight, flat_latent, preferred_element_type=jnp.float32).astype(
        jnp.bfloat16
    )
    fields = jnp.stack([predicted.reshape(channels, latitude_rows, NLON), target])
    harmonic_basis = fourier_table(slot_ids)
    fourier_modes = jnp.einsum(
        "fclk,kqm->mfqcl", fields, harmonic_basis, preferred_element_type=jnp.float32
    )
    fourier_modes = fourier_modes.astype(jnp.bfloat16).reshape(MPAD, 4 * channels, latitude_rows)
    columns = lax.all_to_all(fourier_modes, "band", split_axis=0, concat_axis=2, tiled=True)
    lat_count = columns.shape[2]
    tables = legendre_rows(resident_orders, lat_count, NLP, TRUNC)
    coefficients = jnp.einsum("tmj,mcj->mct", tables, columns, preferred_element_type=jnp.float32)
    coefficients = coefficients.reshape(band_partition, 2, 2, channels, NLP)
    pred_coef = coefficients[:, 0]
    true_coef = coefficients[:, 1]
    spectra_local = jnp.concatenate(
        [
            jnp.sum(pred_coef * pred_coef, axis=1),
            jnp.sum(true_coef * true_coef, axis=1),
            jnp.sum(pred_coef * true_coef, axis=1),
        ],
        axis=1,
    )

    def deposit(slot_id, running):
        first_row = resident_orders[slot_id]
        current = lax.dynamic_slice(running, (0, first_row), (3 * channels, NLP))
        return lax.dynamic_update_slice(running, current + spectra_local[slot_id], (0, first_row))

    by_degree = lax.fori_loop(
        0, band_partition, deposit, jnp.zeros((3 * channels, MPAD + NLP), jnp.float32)
    )
    totals = lax.psum(by_degree[:, :NL], "band")
    loss_terms, d_power, d_cross = spectral_terms(
        totals[:channels], totals[channels : 2 * channels], totals[2 * channels :]
    )
    derivative = jnp.concatenate([d_power, d_cross], axis=0)
    padded = jnp.concatenate(
        [derivative, jnp.zeros((2 * channels, MPAD + NLP - NL), jnp.float32)], axis=1
    )

    def window(first_row):
        return lax.dynamic_slice(padded, (0, first_row), (2 * channels, NLP))

    aligned = jax.vmap(window)(resident_orders)
    gradient = (
        2.0 * aligned[:, None, :channels] * pred_coef + aligned[:, None, channels:] * true_coef
    )
    gradient = gradient.astype(jnp.bfloat16).reshape(band_partition, 2 * channels, NLP)
    inverse_transform = jnp.einsum(
        "tmj,mct->mcj", tables, gradient, preferred_element_type=jnp.float32
    )
    inverse_transform = inverse_transform.astype(jnp.bfloat16)
    rows_back = lax.all_to_all(inverse_transform, "band", split_axis=2, concat_axis=0, tiled=True)
    upstream_gradient = jnp.einsum(
        "mqcj,kqm->cjk",
        rows_back.reshape(MPAD, 2, channels, latitude_rows),
        harmonic_basis,
        preferred_element_type=jnp.float32,
    )
    flat_cot = upstream_gradient.astype(jnp.bfloat16).reshape(channels, cell_count)
    weight_part = lax.dot_general(
        flat_cot, flat_latent, (((1,), (1,)), ((), ())), preferred_element_type=jnp.float32
    )
    grad_weight = lax.psum(weight_part, "band") / math.sqrt(cell_count * bands)
    half_width = latent_width // lax.axis_size("chan")
    latent_sum = lax.psum_scatter(
        lax.dot_general(
            decoder_weight, flat_cot, (((0,), (0,)), ((), ())), preferred_element_type=jnp.float32
        ),
        "chan",
        scatter_dimension=0,
        tiled=True,
    )
    grad_latent = latent_sum.astype(jnp.bfloat16).reshape(half_width, latitude_rows, NLON)
    return (grad_latent, grad_weight, loss_terms)


def solution(mesh):
    return jax.shard_map(
        local,
        mesh=mesh,
        in_specs=(P(None, "band", None), P("chan", None), P("chan", "band", None)),
        out_specs=(P("chan", "band", None), P("chan", None), P("chan", None)),
        check_vma=False,
    )
```

profile of v0, /device:TPU:0, one launch (start us, length us, event | category | flops | bytes accessed | tf_op | source)
XLA Modules:
  0.0 1705.0 jit_solution(17823784879001319433)
XLA Ops:
  7.2 20.3 %select_convert_fusion.2 = (bf16[1440,1,768]{2,0,1:T(8,128)(2,1)}, bf16[1440,1,768]{2,0,1:T(8,128)(2,1)}) fusion(pred[768]{0:T(1024)(128)(4,1)S(1)} %iota_compare_fusion.1), kind=kLoop, calls=%fused_computation.105 | loop fusion | flops 17694720 | bytes 4424448 | tf_op jit(solution)/shard_map/convert
  30.7 3.1 fusion.62
  38.7 3.2 reshape.587
  41.9 8.4 all-to-all-start
  51.3 840.6 %while.39 = (s32[]{:T(128)}, f32[48,48]{1,0:T(8,128)S(1)}, f32[48,48]{1,0:T(8,128)S(1)}, f32[48,48]{1,0:T(8,128)S(1)}, f32[192,4,48,48]{3,2,1,0:T(8,128)}, /*ind...) while((s32[]{:T(128)}, f32[48,48]{1,0:T(8,128)S(1)}, ...), condition=%wide.region_1.2_spmd.clone.clone, body=%wide.region_0.1_spmd.clone.clone.sunk | while | flops 249559 | bytes 334437 | solution.py:62
  891.9 15.4 copy.45
  907.5 3.5 reshape.588
  912.3 9.6 fusion.65
  921.8 13.2 copy.47
  935.0 13.0 multiply_reduce_fusion.2
  948.0 7.8 pad_maximum_fusion
  956.6 340.6 %while.37 = (s32[]{:T(128)}, f32[63,1536]{1,0:T(8,128)}, s32[48]{0:T(128)S(1)}, f32[48,63,768]{2,0,1:T(8,128)}, s32[]{:T(128)}, /*index=5*/s32[]{:T(128)}, s32[]{:T(128)}) while((s32[]{:T(128)}, f32[63,1536]{1,0:T(8,128)}, s32[48]{0:T(128)S(1)}, f32[48,63,768]{2,0,1:T(8,128)}, s32[]{:T(128)}, /*index=5*/s32[]{:T(128)}, s32[]{:T(128)}) %tuple.129), condition=%wide.region_6.7_spmd, body=%wide.region_5.6_spmd.sunk | while | flops 48389 | bytes 1354887 | solution.py:130
  1299.4 104.9 %all-reduce.4.cloned.1.call-done = f32[63,721]{1,0:T(8,128)} async-done(((f32[63,721]{1,0:T(8,128)}), f32[63,721]{1,0:T(8,128)}) %all-reduce.4.cloned.1.call-update) | async-done | bytes 181708 | tf_op jit(solution)/shard_map/psum | solution.py:133
  1406.7 136.0 %while.38 = (s32[]{:T(128)}, f32[42,1536]{1,0:T(8,128)}, s32[48,2]{0,1:T(2,128)S(1)}, f32[48,42,768]{2,1,0:T(8,128)}, s32[]{:T(128)}) while((s32[]{:T(128)}, f32[42,1536]{1,0:T(8,128)}, s32[48,2]{0,1:T(2,128)S(1)}, f32[48,42,768]{2,1,0:T(8,128)}, s32[]{:T(128)}) %tuple.132), condition=%wide.while_cond, body=%wide.while_body.sunk | while | flops 2 | bytes 296025 | solution.py:143
  1407.3 2.3 bitcast_dynamic-update-slice_fusion.2
  1418.7 2.3 bitcast_dynamic-update-slice_fusion.2
  1424.3 2.3 bitcast_dynamic-update-slice_fusion.2
  1427.2 2.3 bitcast_dynamic-update-slice_fusion.2
  1430.0 2.3 bitcast_dynamic-update-slice_fusion.2
  1441.3 2.3 bitcast_dynamic-update-slice_fusion.2
  1447.0 2.3 bitcast_dynamic-update-slice_fusion.2
  1449.9 2.3 bitcast_dynamic-update-slice_fusion.2
  1455.5 2.3 bitcast_dynamic-update-slice_fusion.2
  1458.4 2.3 bitcast_dynamic-update-slice_fusion.2
  1461.2 2.3 bitcast_dynamic-update-slice_fusion.2
  1472.5 2.3 bitcast_dynamic-update-slice_fusion.2
  1475.4 2.3 bitcast_dynamic-update-slice_fusion.2
  1478.2 2.3 bitcast_dynamic-update-slice_fusion.2
  1515.0 2.3 bitcast_dynamic-update-slice_fusion.2
  1517.8 2.3 bitcast_dynamic-update-slice_fusion.2
  1520.7 2.3 bitcast_dynamic-update-slice_fusion.2
  1523.5 2.3 bitcast_dynamic-update-slice_fusion.2
  1529.2 2.3 bitcast_dynamic-update-slice_fusion.2
  1537.7 2.3 bitcast_dynamic-update-slice_fusion.2
  1542.7 6.7 copy.49
  1551.7 2.7 copy.50
  1554.4 9.9 fusion.38
  1564.3 6.3 fusion.56
  1570.6 2.4 copy.52
  1574.7 12.6 all_to_all.33
  1587.3 2.5 reshape.590
  1589.8 2.4 copy.53
  1593.8 3.7 fusion.53
  1600.2 4.6 convolution_bitcast_fusion
  1604.8 8.1 copy.58
  1615.1 74.0 %psum.15 = f32[21,384]{1,0:T(8,128)S(1)} all-reduce(f32[21,384]{1,0:T(8,128)} %convolution_bitcast_fusion.1), channel_id=1, replica_groups=mesh['band'=16,'chan'=2] {'band'}, use_global_device_ids=true, to_apply=%region_9.10 | all-reduce | flops 8064 | bytes 64512 | tf_op jit(solution)/shard_map/psum | solution.py:165
  1689.7 4.5 copy.59
  1694.2 4.0 copy.55
  (1714 shorter events, 713.0 us)
Async XLA Ops:
  7.2 20.3 %copy-start = (bf16[384,3,1440]{0,2,1:T(8,128)(2,1)S(1)}, bf16[384,3,1440]{0,2,1:T(8,128)(2,1)}, u32[]{:S(2)}) copy-start(bf16[384,3,1440]{0,2,1:T(8,128)(2,1)} %param.7) | copy-start | bytes 9953284
  7.2 20.3 %copy-start.4 = (bf16[21,384]{1,0:T(8,128)(2,1)S(1)}, bf16[21,384]{1,0:T(8,128)(2,1)}, u32[]{:S(2)}) copy-start(bf16[21,384]{1,0:T(8,128)(2,1)} %param.8) | copy-start | bytes 48388
  41.9 865.6 %all-to-all-start = ((bf16[16,2,6048]{2,1,0:T(2,128)(2,1)}), bf16[16,2,6048]{2,1,0:T(2,128)(2,1)}, u32[]{:S(2)}, u32[]{:S(2)}) async-start(bf16[16,2,6048]{2,1,0:T(2,128)(2,1)} %reshape.587), calls=%async_computation | async-start | bytes 786432 | tf_op jit(solution)/shard_map/all_to_all | solution.py:109
  50.3 1354.0 %all-reduce.4.cloned.1.call-start = ((), (), s32[]{:S(2)}) async-start(), calls=%async_computation.3 | async-start | bytes 393216 | tf_op jit(solution)/shard_map/psum | solution.py:133
  907.4 14.4 copy-start.5
  1298.8 390.9 %reduce-scatter.4.cloned.1.call-start = ((), (), s32[]{:S(2)}) async-start(), calls=%async_computation.4 | async-start | bytes 10027008
  1542.7 6.8 copy-start.1
  1554.4 9.9 copy-start.6
  1597.5 0.7 copy-start.2
  1612.9 0.9 copy-start.3
Sparse Core Ops, SparseCore 0:
  1298.9 105.3 all-reduce.3
  1613.1 12.5 reduce-scatter.3
where the time goes:
time: 1720 us; the launch traced here: 1710 us
  loops' own time  586 us (34%)
  local copies, waits for them, and re-layouts  549 us (32%)
  other arithmetic  326 us (19%)
  waiting for transfers between devices  105 us (6%)
  blocking collectives  86.6 us (5%)
  matrix products  29.7 us (2%)
    another operation x1, loops' own time, legendre_rows(): _, stacked = lax.scan(advance, initial, jnp.arange(row_total), unroll=4)  494 us
    gather x144, local copies, waits for them, and re-layouts  136 us
    dynamic_update_slice x192, other arithmetic, legendre_rows(): _, stacked = lax.scan(advance, initial, jnp.arange(row_total), unroll=4)  125 us
    slice x192, local copies, waits for them, and re-layouts, legendre_rows(): _, stacked = lax.scan(advance, initial, jnp.arange(row_total), unroll=4)  113 us
    psum x1, waiting for transfers between devices, local(): totals = lax.psum(by_degree[:, :NL], 'band')  105 us
    dynamic_update_slice x48, local copies, waits for them, and re-layouts, deposit(): lax.dynamic_update_slice(running, current + spectra_local[slot_id], (0, f...  92.9 us
    another operation x1, loops' own time, local(): lax.fori_loop(0, band_partition, deposit, jnp.zeros((3 * channels, MPAD +...  91.7 us
    dynamic_slice x48, local copies, waits for them, and re-layouts, deposit(): spectra_local[slot_id]  74 us
  transfers between devices with their start and end apart: 3, of which 1 were waited for; matrix products, arithmetic and copies ran while one was open for 21% of the time, Pallas kernels for 0%

commit v1 on v0

v1 whole, which is shorter than its diff:
```python
import functools
import math

import jax
import jax.numpy as jnp
from jax import lax
from jax.experimental import pallas as pl
from jax.experimental.pallas import tpu as pltpu
from jax.sharding import PartitionSpec as P

NLON = 1440
TRUNC = 720
MPAD = 768
NL = 721
NLP = 768


def fourier_table(order_ids):
    longitude = jnp.arange(NLON)
    phase_index = longitude[:, None] * order_ids[None, :] % NLON
    angles = 2.0 * math.pi / NLON * phase_index.astype(jnp.float32)
    in_range = (order_ids <= TRUNC)[None, :]
    norm_scale = 1.0 / math.sqrt(NLON)
    cosines = jnp.where(in_range, jnp.cos(angles) * norm_scale, 0.0)
    negsines = jnp.where(in_range, -jnp.sin(angles) * norm_scale, 0.0)
    return jnp.stack([cosines, negsines], axis=1).astype(jnp.bfloat16)


def legendre_kernel(cutoff, step_rows, order_ref, start_ref, cos_ref, weight_ref, out_ref, before_ref, current_ref, scale_ref):
    step = pl.program_id(0)

    @pl.when(step == 0)
    def _():
        before_ref[...] = jnp.zeros_like(before_ref)
        current_ref[...] = jnp.ones_like(current_ref)
        scale_ref[...] = start_ref[...]

    order = order_ref[...]
    cosines = cos_ref[...]
    weights = weight_ref[...]
    squared = order * order
    before = before_ref[...]
    current = current_ref[...]
    log_scale = scale_ref[...]
    for row in range(step_rows):
        previous = order + (step * step_rows + row).astype(jnp.float32)
        degree = previous + 1.0
        value = current * jnp.exp(log_scale) * weights
        out_ref[row] = jnp.where(previous <= cutoff, value, 0.0).astype(out_ref.dtype)
        factor = jnp.sqrt((4.0 * degree * degree - 1.0) / (degree * degree - squared))
        back_factor = jnp.sqrt(
            jnp.maximum(previous * previous - squared, 1e-30)
            / jnp.abs(4.0 * previous * previous - 1.0)
        )
        following = factor * (cosines * current - back_factor * before)
        length = current * current + following * following
        inverse = lax.rsqrt(length)
        before = current * inverse
        current = following * inverse
        log_scale = log_scale + 0.5 * jnp.log(length)
    before_ref[...] = before
    current_ref[...] = current
    scale_ref[...] = log_scale


def legendre_rows(order_ids, lat_count, row_total, cutoff):
    lat_index = jnp.arange(lat_count).astype(jnp.float32)
    colatitude = math.pi * (lat_index + 0.5) / lat_count
    cosines = jnp.cos(colatitude)
    colat_sin = jnp.sin(colatitude)
    weights = math.sqrt(math.pi / lat_count) * colat_sin
    order_float = order_ids.astype(jnp.float32)[:, None]
    log_start = (
        0.5 * jnp.log(order_float + 0.5)
        + lax.lgamma(order_float + 0.5)
        - lax.lgamma(order_float + 1.0)
        - 0.5 * math.log(math.pi)
        + order_float * jnp.log(colat_sin)[None, :]
    )
    shape = log_start.shape
    operands = [
        jnp.broadcast_to(order_float, shape),
        log_start,
        jnp.broadcast_to(cosines[None, :], shape),
        jnp.broadcast_to(weights[None, :], shape),
    ]
    step_rows = 16
    return pl.pallas_call(
        functools.partial(legendre_kernel, float(cutoff), step_rows),
        grid=(row_total // step_rows,),
        out_shape=jax.ShapeDtypeStruct((row_total,) + shape, jnp.bfloat16),
        in_specs=[pl.BlockSpec(shape, lambda i: (0, 0))] * 4,
        out_specs=pl.BlockSpec((step_rows,) + shape, lambda i: (i, 0, 0)),
        scratch_shapes=[pltpu.VMEM(shape, jnp.float32)] * 3,
        name="legendre",
    )(*operands)


def analyse_kernel(rows, width, table_ref, columns_ref, out_ref):
    slot = pl.program_id(0)

    @pl.when(slot == 0)
    def _():
        out_ref[...] = jnp.zeros_like(out_ref)

    coef = jnp.dot(columns_ref[0], table_ref[0], preferred_element_type=jnp.float32)
    p0, p1, t0, t1 = (coef[i * rows : (i + 1) * rows] for i in range(4))
    spectra = jnp.concatenate([p0 * p0 + p1 * p1, t0 * t0 + t1 * t1, p0 * t0 + p1 * t1], axis=0)
    spare = jnp.zeros((3 * rows, width - spectra.shape[1]), jnp.float32)
    out_ref[...] += pltpu.roll(jnp.concatenate([spectra, spare], axis=1), slot, 1)


def synthesise_kernel(rows, width, table_ref, columns_ref, derivative_ref, out_ref):
    slot = pl.program_id(0)
    table = table_ref[0]
    coef = jnp.dot(columns_ref[0], table, preferred_element_type=jnp.float32)
    p0, p1, t0, t1 = (coef[i * rows : (i + 1) * rows] for i in range(4))
    aligned = pltpu.roll(derivative_ref[...], width - slot, 1)[:, : table.shape[1]]
    d_power, d_cross = 2.0 * aligned[:rows], aligned[rows:]
    gradient = jnp.concatenate([d_power * p0 + d_cross * t0, d_power * p1 + d_cross * t1], axis=0)
    out_ref[0] = lax.dot_general(
        gradient.astype(jnp.bfloat16),
        table,
        (((1,), (1,)), ((), ())),
        preferred_element_type=jnp.float32,
    ).astype(out_ref.dtype)


def spectral_terms(power_pred, power_true, cross_power):
    first_power = power_pred + 1.0
    second_power = power_true + 1.0
    first_root = jnp.sqrt(first_power)
    second_root = jnp.sqrt(second_power)
    joint_root = first_root * second_root
    coherence = cross_power / joint_root
    combined = first_power + second_power
    loss_terms = jnp.square(first_root - second_root) + combined * (1.0 - coherence)
    d_power = (
        2.0
        - second_root / first_root
        - coherence
        + combined * cross_power / (2.0 * first_power * joint_root)
    )
    d_cross = -combined / joint_root
    return (loss_terms, d_power, d_cross)


def local(latent, decoder_weight, target):
    bands = lax.axis_size("band")
    band_index = lax.axis_index("band")
    band_partition = MPAD // bands
    latitude_rows = target.shape[1]
    channels = target.shape[0]
    latent_width = latent.shape[0]
    cell_count = latitude_rows * NLON
    slot_ids = jnp.arange(MPAD)
    resident_orders = lax.dynamic_slice_in_dim(
        slot_ids, band_index * band_partition, band_partition, 0
    )
    flat_latent = latent.reshape(latent_width, cell_count)
    predicted = jnp.dot(decoder_weight, flat_latent, preferred_element_type=jnp.float32).astype(
        jnp.bfloat16
    )
    fields = jnp.stack([predicted.reshape(channels, latitude_rows, NLON), target])
    harmonic_basis = fourier_table(slot_ids)
    fourier_modes = jnp.einsum(
        "fclk,kqm->mfqcl", fields, harmonic_basis, preferred_element_type=jnp.float32
    )
    fourier_modes = fourier_modes.astype(jnp.bfloat16).reshape(MPAD, 4 * channels, latitude_rows)
    columns = lax.all_to_all(fourier_modes, "band", split_axis=0, concat_axis=2, tiled=True)
    lat_count = columns.shape[2]
    tables = legendre_rows(resident_orders, lat_count, NLP, TRUNC).transpose(1, 2, 0)
    rows = -(-channels // 8) * 8
    width = NLP + -(-band_partition // 128) * 128
    padded_columns = jnp.pad(
        columns.reshape(band_partition, 4, channels, lat_count),
        ((0, 0), (0, 0), (0, rows - channels), (0, 0)),
    ).reshape(band_partition, 4 * rows, lat_count)
    table_spec = pl.BlockSpec((1, lat_count, NLP), lambda i: (i, 0, 0))
    column_spec = pl.BlockSpec((1, 4 * rows, lat_count), lambda i: (i, 0, 0))
    first_order = band_index * band_partition
    spectra_local = pl.pallas_call(
        functools.partial(analyse_kernel, rows, width),
        grid=(band_partition,),
        out_shape=jax.ShapeDtypeStruct((3 * rows, width), jnp.float32),
        in_specs=[table_spec, column_spec],
        out_specs=pl.BlockSpec((3 * rows, width), lambda i: (0, 0)),
        name="analyse",
    )(tables, padded_columns)
    by_degree = lax.dynamic_update_slice(
        jnp.zeros((3 * rows, MPAD + width), jnp.float32), spectra_local, (0, first_order)
    )
    by_degree = by_degree.reshape(3, rows, MPAD + width)[:, :channels, :NL]
    totals = lax.psum(by_degree.reshape(3 * channels, NL), "band")
    loss_terms, d_power, d_cross = spectral_terms(
        totals[:channels], totals[channels : 2 * channels], totals[2 * channels :]
    )
    derivative = jnp.pad(
        jnp.stack([d_power, d_cross]),
        ((0, 0), (0, rows - channels), (0, MPAD + width - NL)),
    ).reshape(2 * rows, MPAD + width)
    derivative = lax.dynamic_slice(derivative, (0, first_order), (2 * rows, width))
    inverse_transform = pl.pallas_call(
        functools.partial(synthesise_kernel, rows, width),
        grid=(band_partition,),
        out_shape=jax.ShapeDtypeStruct((band_partition, 2 * rows, lat_count), jnp.bfloat16),
        in_specs=[
            table_spec,
            column_spec,
            pl.BlockSpec((2 * rows, width), lambda i: (0, 0)),
        ],
        out_specs=pl.BlockSpec((1, 2 * rows, lat_count), lambda i: (i, 0, 0)),
        name="synthesise",
    )(tables, padded_columns, derivative)
    inverse_transform = inverse_transform.reshape(band_partition, 2, rows, lat_count)[
        :, :, :channels
    ].reshape(band_partition, 2 * channels, lat_count)
    rows_back = lax.all_to_all(inverse_transform, "band", split_axis=2, concat_axis=0, tiled=True)
    upstream_gradient = jnp.einsum(
        "mqcj,kqm->cjk",
        rows_back.reshape(MPAD, 2, channels, latitude_rows),
        harmonic_basis,
        preferred_element_type=jnp.float32,
    )
    flat_cot = upstream_gradient.astype(jnp.bfloat16).reshape(channels, cell_count)
    weight_part = lax.dot_general(
        flat_cot, flat_latent, (((1,), (1,)), ((), ())), preferred_element_type=jnp.float32
    )
    grad_weight = lax.psum(weight_part, "band") / math.sqrt(cell_count * bands)
    half_width = latent_width // lax.axis_size("chan")
    half_weight = lax.dynamic_slice_in_dim(
        lax.all_gather(decoder_weight, "chan", axis=0, tiled=True),
        lax.axis_index("chan") * half_width,
        half_width,
        1,
    )
    latent_sum = lax.dot_general(
        half_weight,
        lax.all_gather(flat_cot, "chan", axis=0, tiled=True),
        (((0,), (0,)), ((), ())),
        preferred_element_type=jnp.float32,
    )
    grad_latent = latent_sum.astype(jnp.bfloat16).reshape(half_width, latitude_rows, NLON)
    return (grad_latent, grad_weight, loss_terms)


def solution(mesh):
    return jax.shard_map(
        local,
        mesh=mesh,
        in_specs=(P(None, "band", None), P("chan", None), P("chan", "band", None)),
        out_specs=(P("chan", "band", None), P("chan", None), P("chan", None)),
        check_vma=False,
    )
```

time: 1720 us -> 426 us (0.25)
  loops' own time: 586 us -> 0 us
  local copies, waits for them, and re-layouts: 549 us -> 71 us
  other arithmetic: 326 us -> 23.5 us
  Pallas kernels: 0 us -> 96.2 us
  matrix products: 29.7 us -> 12.2 us
    another operation x3 -> x0, loops' own time: 586 us -> none  [the longest x1 494 us: legendre_rows(): _, stacked = lax.scan(advance, initial, jnp.arange(row_total), unroll=4)]
    gather x145 -> x0, local copies, waits for them, and re-layouts: 143 us -> none
    dynamic_update_slice x192 -> x0, other arithmetic: 125 us -> none  [legendre_rows(): _, stacked = lax.scan(advance, initial, jnp.arange(row_total), unroll=4)]
    dynamic_slice x288 -> x1, local copies, waits for them, and re-layouts: 120 us -> 0.79 us  [local(): lax.dynamic_slice(derivative, (0, first_order), (2 * rows, width))]
    slice x195 -> x1, local copies, waits for them, and re-layouts: 118 us -> 0.95 us  [local(): by_degree = by_degree.reshape(3, rows, MPAD + width)[:, :channels, :NL]]
    pallas_call x0 -> x3, Pallas kernels: none -> 96.2 us  [the longest x1 35.8 us: legendre_rows(): pl.pallas_call(functools.partial(legendre_kernel, float(cutoff), step_row...]
    dynamic_update_slice x48 -> x1, local copies, waits for them, and re-layouts: 92.9 us -> 1.92 us  [local(): lax.dynamic_update_slice(jnp.zeros((3 * rows, MPAD + width), jnp.float32)...]
    add x240 -> x0, other arithmetic: 81.2 us -> none  [the longest x48 51 us: deposit(): current + spectra_local[slot_id]]
  transfers between devices with their start and end apart: 3 -> 3, of which waited for: 1 -> 2; matrix products, arithmetic and copies ran while one was open for 21% -> 4% of each run, Pallas kernels for 0% -> 8%
where the time goes in v1:
time: 426 us; the launch traced here: 422 us
  waiting for transfers between devices  114 us (27%)
  Pallas kernels  96.2 us (23%)
  blocking collectives  77.6 us (18%)
  local copies, waits for them, and re-layouts  71 us (17%)
  other arithmetic  23.5 us (6%)
  between operations  14.2 us (3%)
  starting transfers between devices  13.2 us (3%)
  matrix products  12.2 us (3%)
    psum x1, waiting for transfers between devices, local(): totals = lax.psum(by_degree.reshape(3 * channels, NL), 'band')  108 us
    psum x1, blocking collectives, local(): grad_weight = lax.psum(weight_part, 'band') / math.sqrt(cell_count * bands)  73.3 us
    pallas_call x1, Pallas kernels, legendre_rows(): pl.pallas_call(functools.partial(legendre_kernel, float(cutoff), step_row...  35.8 us
    pallas_call x1, Pallas kernels, local(): pl.pallas_call(functools.partial(synthesise_kernel, rows, width), grid=(b...  30.4 us
    pallas_call x1, Pallas kernels, local(): pl.pallas_call(functools.partial(analyse_kernel, rows, width), grid=(band...  30.1 us
    unnamed x16, local copies, waits for them, and re-layouts  23.1 us
    another operation x1, other arithmetic  20.2 us
    pallas_call x1, local copies, waits for them, and re-layouts, legendre_rows(): pl.pallas_call(functools.partial(legendre_kernel, float(cutoff), step_row...  11.6 us
  transfers between devices with their start and end apart: 3, of which 2 were waited for; matrix products, arithmetic and copies ran while one was open for 4% of the time, Pallas kernels for 8%

profile of v1, /device:TPU:0, one launch (start us, length us, event | category | flops | bytes accessed | tf_op | source)
XLA Modules:
  0.0 421.7 jit_solution(6109479962409453552)
XLA Ops:
  7.2 20.2 %select_convert_fusion.1 = (bf16[1440,1,768]{2,0,1:T(8,128)(2,1)}, bf16[1440,1,768]{2,0,1:T(8,128)(2,1)}) fusion(pred[768]{0:T(1024)(128)(4,1)S(1)} %iota_compare_fusion.2), kind=kLoop, calls=%fused_computation.11 | loop fusion | flops 17694720 | bytes 4424448 | tf_op jit(solution)/shard_map/convert
  27.5 1.2 convolution_convert_fusion.1
  28.7 1.0 stack_reshape.3
  29.7 1.0 copy.21
  30.7 3.1 fusion.18
  33.9 0.8 copy.22
  34.7 1.9 reshape.286
  36.5 2.2 copy.23
  38.7 3.2 reshape.307
  41.9 8.4 %all-to-all-start = ((bf16[16,2,6048]{2,1,0:T(2,128)(2,1)}), bf16[16,2,6048]{2,1,0:T(2,128)(2,1)}, u32[]{:S(2)}, u32[]{:S(2)}) async-start(bf16[16,2,6048]{2,1,0:T(2,128)(2,1)} %reshape.307), calls=%async_computation | async-start | bytes 786432 | tf_op jit(solution)/shard_map/all_to_all | solution.py:170
  50.8 0.7 multiply_add_fusion.1.start_ref
  51.5 0.7 broadcast_in_dim.43.order_ref
  53.4 35.8 %legendre.1 = bf16[768,48,48]{2,1,0:T(8,128)(2,1)} custom-call(f32[48,48]{1,0:T(8,128)} %broadcast_in_dim.43.order_ref, f32[48,48]{1,0:T(8,128)} %multiply_add_fusion.1.start_ref, f32[48,48]{1,0:T(8,128)} %broadcast_in_dim.44.cos_ref, f32[48,48]{1,0:T(8,128)} %broadcast_in_dim.45.weight_ref), custom_call_target="tpu_custom_call" | custom-call | tf_op jit(solution)/shard_map/legendre/pallas_call | solution.py:88
  89.1 11.6 %copy.20 = bf16[768,48,48]{0,2,1:T(8,128)(2,1)} copy(bf16[768,48,48]{2,1,0:T(8,128)(2,1)} %legendre.1) | data formatting | bytes 7077888 | tf_op jit(solution)/shard_map/legendre/pallas_call | solution.py:88
  100.7 3.5 reshape.308
  104.2 2.1 copy.24
  106.3 2.3 copy.25
  108.6 2.8 reshape.287
  111.4 3.5 copy.37
  114.8 2.5 pad.8.clone
  117.4 30.1 %analyse.1 = f32[72,896]{1,0:T(8,128)} custom-call(bf16[48,48,768]{2,1,0:T(8,128)(2,1)} %bitcast.67, bf16[48,96,48]{2,1,0:T(8,128)(2,1)} %bitcast.69), custom_call_target="tpu_custom_call" | custom-call | tf_op jit(solution)/shard_map/analyse/pallas_call | solution.py:182
  147.5 0.8 broadcast_in_dim.48
  148.3 1.9 dynamic_update_slice.3
  150.2 0.9 slice.20
  151.1 0.7 reshape.290
  151.8 108.3 %all-reduce.4.cloned.1.call-done = f32[63,721]{1,0:T(8,128)} async-done(((f32[63,721]{1,0:T(8,128)}), f32[63,721]{1,0:T(8,128)}) %all-reduce.4.cloned.1.call-update) | async-done | bytes 181708 | tf_op jit(solution)/shard_map/psum | solution.py:194
  260.2 1.7 multiply_add_fusion
  261.9 0.8 constant_dynamic-slice_fusion.derivative_ref
  262.7 30.4 %synthesise.1 = bf16[48,48,48]{2,1,0:T(8,128)(2,1)} custom-call(bf16[48,48,768]{2,1,0:T(8,128)(2,1)} %bitcast.68, bf16[48,96,48]{2,1,0:T(8,128)(2,1)} %bitcast.70, f32[48,896]{1,0:T(8,128)} %constant_dynamic-slice_fusion.derivative_ref), custom_call_target="tpu_custom_call" | custom-call | tf_op jit(solution)/shard_map/synthesise/pallas_call | solution.py:203
  293.1 2.0 copy.36
  295.1 2.3 copy.28
  297.4 2.4 reshape.309
  299.8 4.6 %all-to-all-start.1 = ((bf16[16,2,3024]{2,1,0:T(2,128)(2,1)}), bf16[16,2,3024]{2,1,0:T(2,128)(2,1)S(1)}, u32[]{:S(2)}, u32[]{:S(2)}) async-start(bf16[16,2,3024]{2,1,0:T(2,128)(2,1)} %reshape.309), calls=%async_computation.1 | async-start | bytes 393216 | tf_op jit(solution)/shard_map/all_to_all | solution.py:218
  304.4 2.0 all-gather
  307.1 5.4 %all-to-all-done.1 = bf16[16,2,3024]{2,1,0:T(2,128)(2,1)S(1)} async-done(((bf16[16,2,3024]{2,1,0:T(2,128)(2,1)}), bf16[16,2,3024]{2,1,0:T(2,128)(2,1)S(1)}, u32[]{:S(2)}, u32[]{:S(2)}) %all-to-all-start.1) | async-done | bytes 193568 | tf_op jit(solution)/shard_map/all_to_all | solution.py:218
  312.5 1.6 reshape.310
  314.1 2.0 copy.30
  316.1 1.6 reshape.294
  317.7 3.7 fusion.12
  321.4 0.8 copy.31
  322.3 1.2 convolution_bitcast_fusion
  323.5 1.2 reshape.299
  324.7 2.2 all-gather.1
  326.9 1.9 reshape.300
  328.8 2.9 convolution_convert_fusion
  331.7 6.0 %reshape.296 = bf16[192,3,1440]{2,1,0:T(4,128)(2,1)} reshape(bf16[192,4320]{1,0:T(8,128)(2,1)} %convolution_convert_fusion) | data formatting | bytes 3317760 | tf_op jit(solution)/shard_map/reshape | solution.py:243
  337.7 3.2 copy.32
  340.9 73.3 %psum.15 = f32[21,384]{1,0:T(8,128)S(1)} all-reduce(f32[21,384]{1,0:T(8,128)S(1)} %copy-done.1), channel_id=1, replica_groups=mesh['band'=16,'chan'=2] {'band'}, use_global_device_ids=true, to_apply=%region_1.2 | all-reduce | flops 8064 | bytes 64512 | tf_op jit(solution)/shard_map/psum | solution.py:229
  (19 shorter events, 3.0 us)
Async XLA Ops:
  7.2 20.3 %copy-start = (bf16[384,3,1440]{0,2,1:T(8,128)(2,1)S(1)}, bf16[384,3,1440]{0,2,1:T(8,128)(2,1)}, u32[]{:S(2)}) copy-start(bf16[384,3,1440]{0,2,1:T(8,128)(2,1)} %param.3) | copy-start | bytes 9953284
  7.2 20.3 %copy-start.2 = (bf16[21,384]{1,0:T(8,128)(2,1)S(1)}, bf16[21,384]{1,0:T(8,128)(2,1)}, u32[]{:S(2)}) copy-start(bf16[21,384]{1,0:T(8,128)(2,1)} %param.4) | copy-start | bytes 48388
  41.9 58.8 %all-to-all-start = ((bf16[16,2,6048]{2,1,0:T(2,128)(2,1)}), bf16[16,2,6048]{2,1,0:T(2,128)(2,1)}, u32[]{:S(2)}, u32[]{:S(2)}) async-start(bf16[16,2,6048]{2,1,0:T(2,128)(2,1)} %reshape.307), calls=%async_computation | async-start | bytes 786432 | tf_op jit(solution)/shard_map/all_to_all | solution.py:170
  50.3 209.9 %all-reduce.4.cloned.1.call-start = ((), (), s32[]{:S(2)}) async-start(), calls=%async_computation.2 | async-start | bytes 393216 | tf_op jit(solution)/shard_map/psum | solution.py:194
  299.8 12.7 %all-to-all-start.1 = ((bf16[16,2,3024]{2,1,0:T(2,128)(2,1)}), bf16[16,2,3024]{2,1,0:T(2,128)(2,1)S(1)}, u32[]{:S(2)}, u32[]{:S(2)}) async-start(bf16[16,2,3024]{2,1,0:T(2,128)(2,1)} %reshape.309), calls=%async_computation.1 | async-start | bytes 393216 | tf_op jit(solution)/shard_map/all_to_all | solution.py:218
  331.7 9.2 %copy-start.1 = (f32[21,384]{1,0:T(8,128)S(1)}, f32[21,384]{1,0:T(8,128)}, u32[]{:S(2)}) copy-start(f32[21,384]{1,0:T(8,128)} %convolution_bitcast_fusion) | copy-start | bytes 96772
Sparse Core Ops, SparseCore 0:
  152.0 108.1 all-reduce.3

commit v2 on v1

--- a/solution.py
+++ b/solution.py
@@ -16,14 +16,34 @@
 
 
 def fourier_table(order_ids):
-    longitude = jnp.arange(NLON)
-    phase_index = longitude[:, None] * order_ids[None, :] % NLON
-    angles = 2.0 * math.pi / NLON * phase_index.astype(jnp.float32)
-    in_range = (order_ids <= TRUNC)[None, :]
-    norm_scale = 1.0 / math.sqrt(NLON)
-    cosines = jnp.where(in_range, jnp.cos(angles) * norm_scale, 0.0)
-    negsines = jnp.where(in_range, -jnp.sin(angles) * norm_scale, 0.0)
-    return jnp.stack([cosines, negsines], axis=1).astype(jnp.bfloat16)
+    fine_count = 40
+
+    def parts(longitude):
+        phase_index = longitude[:, None] * order_ids[None, :] % NLON
+        angles = 2.0 * math.pi / NLON * phase_index.astype(jnp.float32)
+        return jnp.cos(angles), jnp.sin(angles)
+
+    coarse_cos, coarse_sin = parts(jnp.arange(NLON // fine_count) * fine_count)
+    fine_cos, fine_sin = parts(jnp.arange(fine_count))
+    scale = jnp.where(order_ids <= TRUNC, 1.0 / math.sqrt(NLON), 0.0)[None, :]
+    coarse_cos, coarse_sin, fine_cos, fine_sin = lax.optimization_barrier(
+        (coarse_cos * scale, coarse_sin * scale, fine_cos, fine_sin)
+    )
+    cosines = coarse_cos[:, None] * fine_cos[None] - coarse_sin[:, None] * fine_sin[None]
+    sines = coarse_sin[:, None] * fine_cos[None] + coarse_cos[:, None] * fine_sin[None]
+    shape = (NLON, order_ids.shape[0])
+    basis = jnp.stack([cosines.reshape(shape), -sines.reshape(shape)], axis=1)
+    return basis.astype(jnp.bfloat16)
+
+
+def band_scatter_sum(pieces):
+    return jnp.sum(lax.all_to_all(pieces, "band", split_axis=0, concat_axis=0, tiled=True), axis=0)
+
+
+def band_spread(piece):
+    bands = lax.axis_size("band")
+    copies = jnp.broadcast_to(piece[None], (bands,) + piece.shape)
+    return lax.all_to_all(copies, "band", split_axis=0, concat_axis=0, tiled=True)
 
 
 def legendre_kernel(cutoff, step_rows, order_ref, start_ref, cos_ref, weight_ref, out_ref, before_ref, current_ref, scale_ref):
@@ -96,34 +116,43 @@
     )(*operands)
 
 
-def analyse_kernel(rows, width, table_ref, columns_ref, out_ref):
-    slot = pl.program_id(0)
-
-    @pl.when(slot == 0)
+def analyse_kernel(group, rows, width, table_ref, columns_ref, out_ref):
+    step = pl.program_id(0)
+
+    @pl.when(step == 0)
     def _():
         out_ref[...] = jnp.zeros_like(out_ref)
 
-    coef = jnp.dot(columns_ref[0], table_ref[0], preferred_element_type=jnp.float32)
-    p0, p1, t0, t1 = (coef[i * rows : (i + 1) * rows] for i in range(4))
-    spectra = jnp.concatenate([p0 * p0 + p1 * p1, t0 * t0 + t1 * t1, p0 * t0 + p1 * t1], axis=0)
-    spare = jnp.zeros((3 * rows, width - spectra.shape[1]), jnp.float32)
-    out_ref[...] += pltpu.roll(jnp.concatenate([spectra, spare], axis=1), slot, 1)
-
-
-def synthesise_kernel(rows, width, table_ref, columns_ref, derivative_ref, out_ref):
-    slot = pl.program_id(0)
-    table = table_ref[0]
-    coef = jnp.dot(columns_ref[0], table, preferred_element_type=jnp.float32)
-    p0, p1, t0, t1 = (coef[i * rows : (i + 1) * rows] for i in range(4))
-    aligned = pltpu.roll(derivative_ref[...], width - slot, 1)[:, : table.shape[1]]
-    d_power, d_cross = 2.0 * aligned[:rows], aligned[rows:]
-    gradient = jnp.concatenate([d_power * p0 + d_cross * t0, d_power * p1 + d_cross * t1], axis=0)
-    out_ref[0] = lax.dot_general(
-        gradient.astype(jnp.bfloat16),
-        table,
-        (((1,), (1,)), ((), ())),
-        preferred_element_type=jnp.float32,
-    ).astype(out_ref.dtype)
+    total = out_ref[...]
+    for g in range(group):
+        coef = jnp.dot(columns_ref[g], table_ref[g], preferred_element_type=jnp.float32)
+        p0, p1, t0, t1 = (coef[i * rows : (i + 1) * rows] for i in range(4))
+        spectra = jnp.concatenate(
+            [p0 * p0 + p1 * p1, t0 * t0 + t1 * t1, p0 * t0 + p1 * t1], axis=0
+        )
+        spare = jnp.zeros((3 * rows, width - spectra.shape[1]), jnp.float32)
+        total += pltpu.roll(jnp.concatenate([spectra, spare], axis=1), step * group + g, 1)
+    out_ref[...] = total
+
+
+def synthesise_kernel(group, rows, width, table_ref, columns_ref, derivative_ref, out_ref):
+    step = pl.program_id(0)
+    for g in range(group):
+        table = table_ref[g]
+        coef = jnp.dot(columns_ref[g], table, preferred_element_type=jnp.float32)
+        p0, p1, t0, t1 = (coef[i * rows : (i + 1) * rows] for i in range(4))
+        aligned = pltpu.roll(derivative_ref[...], width - (step * group + g), 1)
+        aligned = aligned[:, : table.shape[1]]
+        d_power, d_cross = 2.0 * aligned[:rows], aligned[rows:]
+        gradient = jnp.concatenate(
+            [d_power * p0 + d_cross * t0, d_power * p1 + d_cross * t1], axis=0
+        )
+        out_ref[g] = lax.dot_general(
+            gradient.astype(jnp.bfloat16),
+            table,
+            (((1,), (1,)), ((), ())),
+            preferred_element_type=jnp.float32,
+        ).astype(out_ref.dtype)
 
 
 def spectral_terms(power_pred, power_true, cross_power):
@@ -176,12 +205,13 @@
         columns.reshape(band_partition, 4, channels, lat_count),
         ((0, 0), (0, 0), (0, rows - channels), (0, 0)),
     ).reshape(band_partition, 4 * rows, lat_count)
-    table_spec = pl.BlockSpec((1, lat_count, NLP), lambda i: (i, 0, 0))
-    column_spec = pl.BlockSpec((1, 4 * rows, lat_count), lambda i: (i, 0, 0))
+    group = next(g for g in (8, 6, 4, 3, 2, 1) if band_partition % g == 0)
+    table_spec = pl.BlockSpec((group, lat_count, NLP), lambda i: (i, 0, 0))
+    column_spec = pl.BlockSpec((group, 4 * rows, lat_count), lambda i: (i, 0, 0))
     first_order = band_index * band_partition
     spectra_local = pl.pallas_call(
-        functools.partial(analyse_kernel, rows, width),
-        grid=(band_partition,),
+        functools.partial(analyse_kernel, group, rows, width),
+        grid=(band_partition // group,),
         out_shape=jax.ShapeDtypeStruct((3 * rows, width), jnp.float32),
         in_specs=[table_spec, column_spec],
         out_specs=pl.BlockSpec((3 * rows, width), lambda i: (0, 0)),
@@ -190,26 +220,25 @@
     by_degree = lax.dynamic_update_slice(
         jnp.zeros((3 * rows, MPAD + width), jnp.float32), spectra_local, (0, first_order)
     )
-    by_degree = by_degree.reshape(3, rows, MPAD + width)[:, :channels, :NL]
-    totals = lax.psum(by_degree.reshape(3 * channels, NL), "band")
-    loss_terms, d_power, d_cross = spectral_terms(
-        totals[:channels], totals[channels : 2 * channels], totals[2 * channels :]
-    )
-    derivative = jnp.pad(
-        jnp.stack([d_power, d_cross]),
-        ((0, 0), (0, rows - channels), (0, MPAD + width - NL)),
-    ).reshape(2 * rows, MPAD + width)
+    pieces = by_degree[:, :MPAD].reshape(3 * rows, bands, band_partition).transpose(1, 0, 2)
+    totals = band_scatter_sum(pieces.reshape(bands, 3 * rows * band_partition))
+    totals = totals.reshape(3, rows * band_partition)
+    terms = jnp.stack(spectral_terms(totals[0], totals[1], totals[2])).reshape(-1)
+    terms = band_spread(terms).reshape(bands, 3 * rows, band_partition)
+    terms = terms.transpose(1, 0, 2).reshape(3 * rows, MPAD)
+    loss_terms = terms[:channels, :NL]
+    derivative = jnp.pad(terms[rows:, :NL], ((0, 0), (0, MPAD + width - NL)))
     derivative = lax.dynamic_slice(derivative, (0, first_order), (2 * rows, width))
     inverse_transform = pl.pallas_call(
-        functools.partial(synthesise_kernel, rows, width),
-        grid=(band_partition,),
+        functools.partial(synthesise_kernel, group, rows, width),
+        grid=(band_partition // group,),
         out_shape=jax.ShapeDtypeStruct((band_partition, 2 * rows, lat_count), jnp.bfloat16),
         in_specs=[
             table_spec,
             column_spec,
             pl.BlockSpec((2 * rows, width), lambda i: (0, 0)),
         ],
-        out_specs=pl.BlockSpec((1, 2 * rows, lat_count), lambda i: (i, 0, 0)),
+        out_specs=pl.BlockSpec((group, 2 * rows, lat_count), lambda i: (i, 0, 0)),
         name="synthesise",
     )(tables, padded_columns, derivative)
     inverse_transform = inverse_transform.reshape(band_partition, 2, rows, lat_count)[
@@ -226,7 +255,11 @@
     weight_part = lax.dot_general(
         flat_cot, flat_latent, (((1,), (1,)), ((), ())), preferred_element_type=jnp.float32
     )
-    grad_weight = lax.psum(weight_part, "band") / math.sqrt(cell_count * bands)
+    weight_size = channels * latent_width
+    weight_pad = -weight_size % bands
+    weight_pieces = jnp.pad(weight_part.reshape(-1), (0, weight_pad)).reshape(bands, -1)
+    weight_sum = band_spread(band_scatter_sum(weight_pieces) / math.sqrt(cell_count * bands))
+    grad_weight = weight_sum.reshape(-1)[:weight_size].reshape(channels, latent_width)
     half_width = latent_width // lax.axis_size("chan")
     half_weight = lax.dynamic_slice_in_dim(
         lax.all_gather(decoder_weight, "chan", axis=0, tiled=True),

time: 426 us -> 223 us (0.52)
  waiting for transfers between devices: 114 us -> 4.98 us
  blocking collectives: 77.6 us -> 31.3 us
  Pallas kernels: 96.2 us -> 53.5 us
  local copies, waits for them, and re-layouts: 71 us -> 88.9 us
  other arithmetic: 23.5 us -> 9.32 us
  between operations: 14.2 us -> 0.88 us
  starting transfers between devices: 13.2 us -> 20.8 us
    psum x1 -> x0, waiting for transfers between devices: 108 us -> none  [local(): totals = lax.psum(by_degree.reshape(3 * channels, NL), 'band')]
    psum x1 -> x0, blocking collectives: 73.3 us -> none  [local(): grad_weight = lax.psum(weight_part, 'band') / math.sqrt(cell_count * bands)]
    pallas_call x2, Pallas kernels: 60.5 us -> 17.7 us  [the longest x1 10.2 us: local(): pl.pallas_call(functools.partial(synthesise_kernel, group, rows, width),...]
    all_to_all x0 -> x2, blocking collectives: none -> 26.8 us  [the longest x1 15.1 us: band_scatter_sum(): lax.all_to_all(pieces, 'band', split_axis=0, concat_axis=0, tiled=True)]
    another operation x2, other arithmetic: 20.3 us -> 2.64 us
    all_to_all x0 -> x2, starting transfers between devices: none -> 8.82 us  [the longest x1 5.29 us: band_scatter_sum(): lax.all_to_all(pieces, 'band', split_axis=0, concat_axis=0, tiled=True)]
    unnamed x16 -> x20, local copies, waits for them, and re-layouts: 23.1 us -> 27.2 us
  transfers between devices with their start and end apart: 3 -> 4, of which waited for: 2 -> 2; matrix products, arithmetic and copies ran while one was open for 4% -> 15% of each run, Pallas kernels for 8% -> 16%
where the time goes in v2:
time: 223 us; the launch traced here: 220 us
  local copies, waits for them, and re-layouts  88.9 us (40%)
  Pallas kernels  53.5 us (24%)
  blocking collectives  31.3 us (14%)
  starting transfers between devices  20.8 us (9%)
  matrix products  10.7 us (5%)
  other arithmetic  9.32 us (4%)
  waiting for transfers between devices  4.98 us (2%)
    pallas_call x1, Pallas kernels, legendre_rows(): pl.pallas_call(functools.partial(legendre_kernel, float(cutoff), step_row...  35.8 us
    unnamed x20, local copies, waits for them, and re-layouts  27.2 us
    all_to_all x1, blocking collectives, band_scatter_sum(): lax.all_to_all(pieces, 'band', split_axis=0, concat_axis=0, tiled=True)  15.1 us
    all_to_all x1, blocking collectives, band_spread(): lax.all_to_all(copies, 'band', split_axis=0, concat_axis=0, tiled=True)  11.8 us
    pallas_call x1, local copies, waits for them, and re-layouts, legendre_rows(): pl.pallas_call(functools.partial(legendre_kernel, float(cutoff), step_row...  11.5 us
    pallas_call x1, Pallas kernels, local(): pl.pallas_call(functools.partial(synthesise_kernel, group, rows, width),...  10.2 us
    all_to_all x1, starting transfers between devices, local(): lax.all_to_all(fourier_modes, 'band', split_axis=0, concat_axis=2, tiled=...  8.37 us
    pallas_call x1, Pallas kernels, local(): pl.pallas_call(functools.partial(analyse_kernel, group, rows, width), gri...  7.5 us
  transfers between devices with their start and end apart: 4, of which 2 were waited for; matrix products, arithmetic and copies ran while one was open for 15% of the time, Pallas kernels for 16%

profile of v2, /device:TPU:0, one launch (start us, length us, event | category | flops | bytes accessed | tf_op | source)
XLA Modules:
  0.0 220.3 jit_solution(16875340893211901734)
XLA Ops:
  0.7 1.2 fusion.24
  1.9 1.3 sine_multiply_fusion
  3.2 2.0 convolution_convert_fusion.1
  7.2 2.6 %subtract_convert_fusion = (bf16[36,40,768]{2,1,0:T(8,128)(2,1)S(1)}, bf16[36,40,768]{2,1,0:T(8,128)(2,1)S(1)}) fusion(f32[40,768]{1,0:T(8,128)} %get-tuple-element.10, f32[36,768]{1,0:T(8,128)} %get-tuple-element.9, f32[40,768]{1,0:T(8,128)} %get-tuple-element.8, f32[36,768]{1,0:T(8,128)} %get-tuple-element.7), kind=kLoop, calls=%fused_computation.8 | loop fusion | flops 9953280 | bytes 4890624 | tf_op jit(solution)/shard_map/convert.3
  12.7 1.9 reshape.338
  14.6 2.2 copy.28
  16.7 3.2 %reshape.361 = bf16[16,2,6048]{2,1,0:T(2,128)(2,1)} reshape(bf16[768,3,84]{2,1,0:T(4,128)(2,1)} %bitcast.74) | data formatting | bytes 774144
  19.9 8.4 %all-to-all-start = ((bf16[16,2,6048]{2,1,0:T(2,128)(2,1)}), bf16[16,2,6048]{2,1,0:T(2,128)(2,1)}, u32[]{:S(2)}, u32[]{:S(2)}) async-start(bf16[16,2,6048]{2,1,0:T(2,128)(2,1)} %reshape.361), calls=%async_computation | async-start | bytes 786432 | tf_op jit(solution)/shard_map/all_to_all | solution.py:199
  31.2 35.8 %legendre.1 = bf16[768,48,48]{2,1,0:T(8,128)(2,1)} custom-call(f32[48,48]{1,0:T(8,128)} %broadcast_in_dim.22.order_ref, f32[48,48]{1,0:T(8,128)} %multiply_add_fusion.start_ref, f32[48,48]{1,0:T(8,128)} %broadcast_in_dim.23.cos_ref, f32[48,48]{1,0:T(8,128)} %broadcast_in_dim.24.weight_ref), custom_call_target="tpu_custom_call" | custom-call | tf_op jit(solution)/shard_map/legendre/pallas_call | solution.py:108
  67.0 11.5 %copy.25 = bf16[768,48,48]{0,2,1:T(8,128)(2,1)} copy(bf16[768,48,48]{2,1,0:T(8,128)(2,1)} %legendre.1) | data formatting | bytes 7077888 | tf_op jit(solution)/shard_map/legendre/pallas_call | solution.py:108
  78.5 3.5 %reshape.362 = bf16[768,3,84]{2,1,0:T(4,128)(2,1)} reshape(bf16[16,2,6048]{2,1,0:T(2,128)(2,1)} %all-to-all-done) | data formatting | bytes 774144
  82.0 2.1 copy.29
  84.0 2.3 %copy.30 = bf16[48,84,16,3]{0,1,3,2:T(8,128)(2,1)} copy(bf16[48,84,16,3]{1,0,2,3:T(8,128)(2,1)} %bitcast.76) | data formatting | bytes 774144 | tf_op jit(solution)/shard_map/all_to_all | solution.py:199
  86.4 2.8 %reshape.339 = bf16[48,4,21,48]{0,2,1,3:T(8,128)(2,1)} reshape(bf16[48,84,16,3]{0,1,3,2:T(8,128)(2,1)} %copy.30) | data formatting | bytes 774144 | tf_op jit(solution)/shard_map/reshape | solution.py:205
  89.1 3.5 %copy.50 = bf16[48,4,21,48]{3,2,1,0:T(8,128)(2,1)} copy(bf16[48,4,21,48]{0,2,1,3:T(8,128)(2,1)} %reshape.339) | data formatting | bytes 774144
  92.6 2.5 %pad.8.clone = bf16[48,4,24,48]{3,2,1,0:T(8,128)(2,1)} pad(bf16[48,4,21,48]{3,2,1,0:T(8,128)(2,1)} %copy.50, bf16[]{:T(256)} %constant.119.clone.1), padding=0_0x0_0x0_3x0_0 | pad | bytes 829442 | tf_op jit(solution)/shard_map/jit(_pad)/pad | solution.py:204
  95.2 7.5 %analyse.1 = f32[72,896]{1,0:T(8,128)} custom-call(bf16[48,48,768]{2,1,0:T(8,128)(2,1)} %bitcast.68, bf16[48,96,48]{2,1,0:T(8,128)(2,1)} %bitcast.70), custom_call_target="tpu_custom_call" | custom-call | tf_op jit(solution)/shard_map/analyse/pallas_call | solution.py:212
  102.7 1.9 copy.32
  106.5 2.0 copy.33
  108.5 1.6 all_to_all.54
  110.2 15.1 %all_to_all.62 = f32[16,1,3456]{2,1,0:T(1,128)} all-to-all(f32[16,1,3456]{2,1,0:T(1,128)S(1)} %all_to_all.54), channel_id=1, replica_groups=mesh['band'=16,'chan'=2] {'band'}, dimensions={0} | all-to-all | bytes 442368 | tf_op jit(solution)/shard_map/all_to_all | solution.py:40
  126.5 11.8 %all_to_all.63 = f32[16,1,3456]{2,1,0:T(1,128)S(1)} all-to-all(f32[16,1,3456]{2,1,0:T(1,128)S(1)} %broadcast_in_dim.29), channel_id=1, replica_groups=mesh['band'=16,'chan'=2] {'band'}, dimensions={0} | all-to-all | bytes 442368 | tf_op jit(solution)/shard_map/all_to_all | solution.py:46
  138.3 1.2 reduce.2
  139.5 2.0 reshape.342
  141.6 2.0 copy.35
  143.6 1.9 slice.35
  147.4 10.2 %synthesise.1 = bf16[48,48,48]{2,1,0:T(8,128)(2,1)} custom-call(bf16[48,48,768]{2,1,0:T(8,128)(2,1)} %bitcast.69, bf16[48,96,48]{2,1,0:T(8,128)(2,1)} %bitcast.71, f32[48,896]{1,0:T(8,128)} %pad_dynamic-slice_fusion.derivative_ref), custom_call_target="tpu_custom_call" | custom-call | tf_op jit(solution)/shard_map/synthesise/pallas_call | solution.py:232
  157.6 2.0 copy.49
  159.6 2.3 %copy.38 = bf16[48,42,48]{0,1,2:T(8,128)(2,1)} copy(bf16[48,42,48]{2,0,1:T(8,128)(2,1)} %bitcast.85) | data formatting | bytes 387072 | tf_op jit(solution)/shard_map/reshape | solution.py:246
  161.9 2.4 %reshape.363 = bf16[16,2,3024]{2,1,0:T(2,128)(2,1)} reshape(bf16[48,42,48]{2,1,0:T(8,128)(2,1)} %bitcast.78) | data formatting | bytes 387072
  164.3 3.6 %all-to-all-start.3 = ((bf16[16,2,3024]{2,1,0:T(2,128)(2,1)}), bf16[16,2,3024]{2,1,0:T(2,128)(2,1)S(1)}, u32[]{:S(2)}, u32[]{:S(2)}) async-start(bf16[16,2,3024]{2,1,0:T(2,128)(2,1)} %reshape.363), calls=%async_computation.3 | async-start | bytes 393216 | tf_op jit(solution)/shard_map/all_to_all | solution.py:247
  167.9 2.3 %all-gather = bf16[2,21,384]{2,1,0:T(8,128)(2,1)S(1)} all-gather(bf16[1,21,384]{2,1,0:T(8,128)(2,1)} %bitcast.87), channel_id=1, replica_groups=mesh['band'=16,'chan'=2] {'chan'}, dimensions={0}, use_global_device_ids=true | all-gather | bytes 48384 | tf_op jit(solution)/shard_map/all_gather | solution.py:265
  170.8 1.8 slice.37
  172.5 1.8 copy.44
  174.3 1.7 all-to-all-done.3
  175.9 1.6 reshape.364
  177.5 2.0 copy.40
  179.5 1.6 reshape.346
  181.2 3.7 %fusion.7 = bf16[21,3,1440]{2,0,1:T(8,128)(2,1)S(1)} fusion(bf16[768,2,21,3]{0,2,1,3:T(8,128)(2,1)S(1)} %reshape.346, bf16[1440,1,768]{2,0,1:T(8,128)(2,1)} %bitcast.84, bf16[1440,1,768]{2,0,1:T(8,128)(2,1)} %bitcast.82), kind=kOutput, calls=%fused_computation.10 | convolution fusion | flops 280994400 | bytes 4798656 | tf_op jit(solution)/shard_map/mqcj,kqm->cjk/dot_general | solution.py:248
  188.1 1.5 all_to_all.55
  189.7 5.3 %all-to-all-start.4 = ((f32[16,1,504]{2,1,0:T(1,128)}), f32[16,1,504]{2,1,0:T(1,128)}, u32[]{:S(2)}, u32[]{:S(2)}) async-start(f32[16,1,504]{2,1,0:T(1,128)} %all_to_all.55), calls=%async_computation.4 | async-start | bytes 65536 | tf_op jit(solution)/shard_map/all_to_all | solution.py:40
  194.9 2.2 %all-gather.1 = bf16[2,21,4320]{2,1,0:T(8,128)(2,1)} all-gather(bf16[1,21,4320]{2,1,0:T(8,128)(2,1)S(1)} %reshape.351), channel_id=1, replica_groups=mesh['band'=16,'chan'=2] {'chan'}, dimensions={0}, use_global_device_ids=true | all-gather | bytes 544320 | tf_op jit(solution)/shard_map/all_gather | solution.py:272
  197.2 1.9 reshape.352
  199.1 3.3 %all-to-all-done.4 = f32[16,1,504]{2,1,0:T(1,128)} async-done(((f32[16,1,504]{2,1,0:T(1,128)}), f32[16,1,504]{2,1,0:T(1,128)}, u32[]{:S(2)}, u32[]{:S(2)}) %all-to-all-start.4) | async-done | bytes 32288 | tf_op jit(solution)/shard_map/all_to_all | solution.py:40
  203.8 3.5 %all-to-all-start.5 = ((f32[16,1,504]{2,1,0:T(1,128)}), f32[16,1,504]{2,1,0:T(1,128)S(1)}, u32[]{:S(2)}, u32[]{:S(2)}) async-start(f32[16,1,504]{2,1,0:T(1,128)} %broadcast_in_dim.30), calls=%async_computation.5 | async-start | bytes 65536 | tf_op jit(solution)/shard_map/all_to_all | solution.py:46
  207.4 2.9 %convolution_convert_fusion = bf16[192,4320]{1,0:T(8,128)(2,1)} fusion(bf16[42,4320]{1,0:T(8,128)(2,1)} %reshape.352, bf16[42,384]{1,0:T(8,128)(2,1)} %reshape.350, s32[]{:T(128)S(6)} %select_n.37), kind=kOutput, calls=%fused_computation | convolution fusion | flops 70502400 | bytes 2101252 | tf_op jit(solution)/shard_map/dot_general | solution.py:270
  210.3 6.0 %reshape.348 = bf16[192,3,1440]{2,1,0:T(4,128)(2,1)} reshape(bf16[192,4320]{1,0:T(8,128)(2,1)} %convolution_convert_fusion) | data formatting | bytes 3317760 | tf_op jit(solution)/shard_map/reshape | solution.py:276
  216.2 3.2 %copy.43 = bf16[192,3,1440]{2,0,1:T(8,128)(2,1)} copy(bf16[192,3,1440]{2,1,0:T(4,128)(2,1)} %reshape.348) | data formatting | bytes 3317760
  (46 shorter events, 18.9 us)
Async XLA Ops:
  0.6 2.6 %copy-start = (bf16[384,3,1440]{0,2,1:T(8,128)(2,1)S(1)}, bf16[384,3,1440]{0,2,1:T(8,128)(2,1)}, u32[]{:S(2)}) copy-start(bf16[384,3,1440]{0,2,1:T(8,128)(2,1)} %param.3) | copy-start | bytes 9953284
  6.2 3.7 %copy-start.3 = (bf16[21,3,1440]{2,0,1:T(8,128)(2,1)S(1)}, bf16[21,3,1440]{2,0,1:T(8,128)(2,1)}, u32[]{:S(2)}) copy-start(bf16[21,3,1440]{2,0,1:T(8,128)(2,1)} %param.5) | copy-start | bytes 544324
  9.9 1.3 copy-start.1
  9.9 2.0 copy-start.2
  19.9 58.5 %all-to-all-start = ((bf16[16,2,6048]{2,1,0:T(2,128)(2,1)}), bf16[16,2,6048]{2,1,0:T(2,128)(2,1)}, u32[]{:S(2)}, u32[]{:S(2)}) async-start(bf16[16,2,6048]{2,1,0:T(2,128)(2,1)} %reshape.361), calls=%async_computation | async-start | bytes 786432 | tf_op jit(solution)/shard_map/all_to_all | solution.py:199
  164.3 11.7 %all-to-all-start.3 = ((bf16[16,2,3024]{2,1,0:T(2,128)(2,1)}), bf16[16,2,3024]{2,1,0:T(2,128)(2,1)S(1)}, u32[]{:S(2)}, u32[]{:S(2)}) async-start(bf16[16,2,3024]{2,1,0:T(2,128)(2,1)} %reshape.363), calls=%async_computation.3 | async-start | bytes 393216 | tf_op jit(solution)/shard_map/all_to_all | solution.py:247
  189.7 12.8 %all-to-all-start.4 = ((f32[16,1,504]{2,1,0:T(1,128)}), f32[16,1,504]{2,1,0:T(1,128)}, u32[]{:S(2)}, u32[]{:S(2)}) async-start(f32[16,1,504]{2,1,0:T(1,128)} %all_to_all.55), calls=%async_computation.4 | async-start | bytes 65536 | tf_op jit(solution)/shard_map/all_to_all | solution.py:40
  203.8 15.6 %all-to-all-start.5 = ((f32[16,1,504]{2,1,0:T(1,128)}), f32[16,1,504]{2,1,0:T(1,128)S(1)}, u32[]{:S(2)}, u32[]{:S(2)}) async-start(f32[16,1,504]{2,1,0:T(1,128)} %broadcast_in_dim.30), calls=%async_computation.5 | async-start | bytes 65536 | tf_op jit(solution)/shard_map/all_to_all | solution.py:46
